TPU v7x, 32 devices: a whole 2x2x4 slice. The times are simulated.
32 devices in a mesh: group: 2 (over x), expert: 16 (over z, y, core).
Axes of the slice: x: 2, y: 2, z: 4, core: 2. Of those that a mesh axis runs over, the one named last changes fastest.
Arguments:
- queries: bfloat16 [512, 4096], P(('group', 'expert')), parts along dimension 0, may hold values from -30 to 30
- fresh_key_rows: bfloat16 [512, 256], P(('group', 'expert')), parts along dimension 0, may hold values from -6 to 6
- fresh_value_rows: bfloat16 [512, 256], P(('group', 'expert')), parts along dimension 0, may hold values from -6 to 6
- key_cache_pages: bfloat16 [1024, 64, 256], P(('group', 'expert')), parts along dimension 0, may hold values from -6 to 6
- value_cache_pages: bfloat16 [1024, 64, 256], P(('group', 'expert')), parts along dimension 0, may hold values from -6 to 6
- sequence_page_table: int32 [32, 16], P(('group', 'expert')), parts along dimension 0, may hold values from 1 to 12, 32 in all within a row
- last_page_fill: int32 [512], P(('group', 'expert')), parts along dimension 0, may hold values from 1 to 64
- local_page_ranking: int32 [32, 32], P(('group', 'expert')), parts along dimension 0, may hold values from 0 to 31, each once within a row
- residual: bfloat16 [512, 4096], P(('group', 'expert')), parts along dimension 0, may hold values from -3 to 3
- out_weight: bfloat16 [4096, 4096], P(None, 'expert'), may hold values from -0.09375 to 0.09375
- norm_gain: bfloat16 [4096], replicated, may hold values from 0.25 to 1.75
- routes: int32 [512, 2], P(('group', 'expert')), parts along dimension 0, may hold values from 0 to 3, all different within a row; in each aligned block of 16 rows (0 to 15, 16 to 31, ...) at most 12 rows name the same one
- route_weight: float32 [512, 2], P(('group', 'expert')), parts along dimension 0, may hold values from 0.1 to 0.5
- w_gate: bfloat16 [16, 4096, 384], P('expert'), may hold values from -0.09375 to 0.09375
- w_up: bfloat16 [16, 4096, 384], P('expert'), may hold values from -0.09375 to 0.09375
- w_down: bfloat16 [16, 384, 4096], P('expert'), may hold values from -0.15625 to 0.15625
Outputs:
- layer_out: bfloat16 [512, 4096], P(('group', 'expert')), parts along dimension 0
There are 2 independent parts, one for each index of `group`. A program takes and returns all parts, laid end to end along the dimension named above; an argument that names none is the same for every part. Nothing has to cross between parts.
Inputs may be any that keep to these rules, and one draw needn't show every extreme that they name: `routes`: each row names 2 different experts. Among the 16 rows of one device no expert is named more than 12 times, and in every draw some device names some expert exactly 12 times. `sequence_page_table`: each row gives the page counts of one device's 16 sequences; they sum to 32, and the largest is exactly 12. `local_page_ranking`: each row lists the 32 local pages of one device once each.
All inputs are finite; a program needn't handle non-finite values.
Results may differ from a plain program's by a relative error of at most 0.008.
Values may be sent and summed in bfloat16 or wider, within the bound.
A program may use at most 128 MiB of HBM per device.

v0:
```python
import math

import jax
import jax.numpy as jnp
from jax import lax
from jax.sharding import PartitionSpec as P

D = 4096
QUERY_HEADS = 32
KEY_VALUE_HEADS = 2
HEAD_SIZE = 128
SHARDS = 4
CAP = 12


def local_attention(
    queries,
    fresh_key_rows,
    fresh_value_rows,
    key_cache_pages,
    value_cache_pages,
    sequence_page_table,
    last_page_fill,
    local_page_ranking,
):
    count_of_rows = queries.shape[0]
    pooled_pages = local_page_ranking.shape[0]
    page_length = key_cache_pages.shape[1]
    query_group_width = QUERY_HEADS // KEY_VALUE_HEADS
    first_page = jnp.cumsum(sequence_page_table) - sequence_page_table
    page_slot = jnp.arange(pooled_pages, dtype=jnp.int32)
    row_ids = jnp.arange(count_of_rows, dtype=jnp.int32)
    inside = (page_slot[:, None] >= first_page[None, :]) & (
        page_slot[:, None] < (first_page + sequence_page_table)[None, :]
    )
    owner_slot = jnp.sum(jnp.where(inside, row_ids[None, :], 0), axis=1)
    index_slot = page_slot - jnp.sum(jnp.where(inside, first_page[None, :], 0), axis=1)
    placed = local_page_ranking[None, :] == page_slot[:, None]
    page_owner = jnp.sum(jnp.where(placed, owner_slot[None, :], 0), axis=1)
    page_index = jnp.sum(jnp.where(placed, index_slot[None, :], 0), axis=1)
    cached = (sequence_page_table - 1) * page_length + last_page_fill
    token_place = (
        page_index[:, None] * page_length + jnp.arange(page_length, dtype=jnp.int32)[None, :]
    )
    visible = (page_owner[None, :, None] == row_ids[:, None, None]) & (
        token_place[None, :, :] < cached[:, None, None]
    )
    visible = visible.reshape(count_of_rows, pooled_pages * page_length)
    score_scale = 1.0 / math.sqrt(HEAD_SIZE)
    query_head_rows = queries.reshape(count_of_rows, KEY_VALUE_HEADS, query_group_width, HEAD_SIZE)
    key_matrix = key_cache_pages.reshape(pooled_pages * page_length, KEY_VALUE_HEADS, HEAD_SIZE)
    value_matrix = value_cache_pages.reshape(pooled_pages * page_length, KEY_VALUE_HEADS, HEAD_SIZE)
    scores = (
        jnp.einsum(
            "rhgd,thd->rhgt", query_head_rows, key_matrix, preferred_element_type=jnp.float32
        )
        * score_scale
    )
    self_score = (
        jnp.einsum(
            "jqnu,jqu->jqn",
            query_head_rows,
            fresh_key_rows.reshape(count_of_rows, KEY_VALUE_HEADS, HEAD_SIZE),
            preferred_element_type=jnp.float32,
        )
        * score_scale
    )
    scores = jnp.where(visible[:, None, None, :], scores, -jnp.inf)
    highest = jnp.maximum(jnp.max(scores, axis=-1), self_score)
    raised = jnp.exp(scores - highest[..., None])
    own_raised = jnp.exp(self_score - highest)
    denominator = jnp.sum(raised, axis=-1) + own_raised
    weights = (raised / denominator[..., None]).astype(jnp.bfloat16)
    self_weight = (own_raised / denominator).astype(jnp.bfloat16)
    mixed_output = jnp.einsum(
        "rhgt,thd->rhgd", weights, value_matrix, preferred_element_type=jnp.float32
    )
    mixed_output = mixed_output + self_weight.astype(jnp.float32)[
        ..., None
    ] * fresh_value_rows.astype(jnp.float32).reshape(count_of_rows, KEY_VALUE_HEADS, 1, HEAD_SIZE)
    return mixed_output.reshape(count_of_rows, QUERY_HEADS * HEAD_SIZE).astype(jnp.bfloat16)


def per_device(
    queries,
    fresh_key_rows,
    fresh_value_rows,
    key_cache_pages,
    value_cache_pages,
    sequence_page_table,
    last_page_fill,
    local_page_ranking,
    residual,
    out_weight,
    norm_gain,
    routes,
    route_weight,
    w_gate,
    w_up,
    w_down,
):
    head_out = local_attention(
        queries,
        fresh_key_rows,
        fresh_value_rows,
        key_cache_pages,
        value_cache_pages,
        sequence_page_table[0],
        last_page_fill,
        local_page_ranking[0],
    )
    spread = jnp.dot(
        lax.all_gather(head_out, "expert", axis=0, tiled=True),
        out_weight,
        preferred_element_type=jnp.float32,
    ).astype(jnp.bfloat16)
    projected = lax.all_to_all(spread, "expert", split_axis=0, concat_axis=1, tiled=True)
    hidden = residual.astype(jnp.float32) + projected.astype(jnp.float32)
    normed = (
        hidden
        * lax.rsqrt(jnp.mean(hidden * hidden, axis=-1, keepdims=True) + 1e-06)
        * norm_gain.astype(jnp.float32)
    ).astype(jnp.bfloat16)
    device_list = lax.axis_size("expert")
    experts = device_list // SHARDS
    count_of_rows = normed.shape[0]
    top_count = routes.shape[1]
    flat_routes = routes.reshape(-1)
    onehot = (flat_routes[:, None] == jnp.arange(experts, dtype=jnp.int32)[None, :]).astype(
        jnp.int32
    )
    counts = jnp.cumsum(onehot, axis=0)
    slot_index = jnp.sum(onehot * (counts - 1), axis=1)
    place_index = flat_routes * CAP + slot_index
    chosen = (jnp.arange(experts * CAP, dtype=jnp.int32)[:, None] == place_index[None, :]).reshape(
        experts * CAP, count_of_rows, top_count
    )
    picked = jnp.any(chosen, axis=2).astype(jnp.bfloat16)
    weighted = jnp.sum(jnp.where(chosen, route_weight[None, :, :], 0.0), axis=2)
    buffer = (
        jnp.dot(picked, normed, preferred_element_type=jnp.float32)
        .astype(jnp.bfloat16)
        .reshape(experts, CAP, D)
    )
    outgoing = jnp.repeat(buffer, SHARDS, axis=0)
    arrived = lax.all_to_all(outgoing, "expert", split_axis=0, concat_axis=0, tiled=True)
    item_count = arrived.shape[1]
    rows_in = arrived.reshape(-1, D)
    gate = jnp.dot(rows_in, w_gate[0], preferred_element_type=jnp.float32)
    upward = jnp.dot(rows_in, w_up[0], preferred_element_type=jnp.float32)
    act = (jax.nn.silu(gate) * upward).astype(jnp.bfloat16)
    output = jnp.dot(act, w_down[0], preferred_element_type=jnp.float32).astype(jnp.bfloat16)
    partial_value = output.reshape(arrived.shape[0], item_count, D)
    returned = lax.all_to_all(partial_value, "expert", split_axis=0, concat_axis=0, tiled=True)
    summed = jnp.sum(returned.reshape(experts, SHARDS, CAP, D).astype(jnp.float32), axis=1)
    mixture = jnp.dot(
        weighted.T,
        summed.reshape(experts * CAP, D),
        precision=lax.Precision.HIGHEST,
        preferred_element_type=jnp.float32,
    )
    return (hidden + mixture).astype(jnp.bfloat16)


def solution(mesh):
    return jax.shard_map(
        per_device,
        mesh=mesh,
        in_specs=(
            P(("group", "expert"), None),
            P(("group", "expert"), None),
            P(("group", "expert"), None),
            P(("group", "expert"), None, None),
            P(("group", "expert"), None, None),
            P(("group", "expert"), None),
            P(("group", "expert")),
            P(("group", "expert"), None),
            P(("group", "expert"), None),
            P(None, "expert"),
            P(),
            P(("group", "expert"), None),
            P(("group", "expert"), None),
            P("expert", None, None),
            P("expert", None, None),
            P("expert", None, None),
        ),
        out_specs=P(("group", "expert"), None),
        check_vma=False,
    )
```

profile of v0, /device:TPU:13, one launch (start us, length us, event | category | flops | bytes accessed | tf_op | source)
XLA Modules:
  0.0 223.3 jit_solution(9157314452106828933)
XLA Ops:
  6.5 0.9 copy.49
  10.4 0.9 copy.68
  11.3 2.2 reshape.156
  14.5 2.2 fusion.38
  16.7 1.9 copy-done.1
  19.3 2.2 reshape.159
  21.5 3.5 %fusion.16 = bf16[16,2,16,128]{3,2,0,1:T(8,128)(2,1)S(1)} fusion(f32[16,2,16,2048]{3,2,0,1:T(8,128)} %copy-done.1, f32[16,2,16]{2,0,1:T(8,128)S(1)} %get-tuple-element.10, f32[16,2,16]{2,0,1:T(8,128)S(1)} %fusion.32, bf16[2048,2,128,1]{2,1,0,3:T(2,128)(2,1)} %bitcast.87, f32[16,2,128]{2,0,1:T(8,128)S(1)} %copy_bitcast_fusion.1, ...), kind=kOutput, calls=%fused_computation.19 | convolution fusion | flops 271777792 | bytes 5396480 | tf_op jit(solution)/shard_map/rhgt,thd->rhgd/dot_general | solution.py:75
  26.5 40.5 %all-gather.2.cloned.1.call-done = bf16[256,4096]{1,0:T(8,128)(2,1)} async-done(((bf16[16,4096]{1,0:T(8,128)(2,1)}), bf16[256,4096]{1,0:T(8,128)(2,1)}) %all-gather.2.cloned.1.call-update) | async-done | bytes 2097168 | tf_op jit(solution)/shard_map/all_gather | solution.py:113
  67.0 3.6 %convolution_convert_fusion.2 = bf16[256,256]{1,0:T(8,128)(2,1)} fusion(bf16[256,4096]{1,0:T(8,128)(2,1)} %all-gather.2.cloned.1.call-done, bf16[4096,256]{1,0:T(8,128)(2,1)} %param.25), kind=kOutput, calls=%fused_computation.20 | convolution fusion | flops 536936448 | bytes 4325376 | tf_op jit(solution)/shard_map/dot_general | solution.py:112
  70.6 5.7 %all-to-all-start = ((bf16[16,16,256]{2,1,0:T(8,128)(2,1)}), bf16[16,16,256]{2,1,0:T(8,128)(2,1)S(1)}, u32[]{:S(2)}, u32[]{:S(2)}) async-start(bf16[16,16,256]{2,1,0:T(8,128)(2,1)} %bitcast.9), calls=%async_computation | async-start | bytes 262144 | tf_op jit(solution)/shard_map/all_to_all | solution.py:117
  77.0 4.5 %all-to-all-done = bf16[16,16,256]{2,1,0:T(8,128)(2,1)S(1)} async-done(((bf16[16,16,256]{2,1,0:T(8,128)(2,1)}), bf16[16,16,256]{2,1,0:T(8,128)(2,1)S(1)}, u32[]{:S(2)}, u32[]{:S(2)}) %all-to-all-start) | async-done | bytes 131104 | tf_op jit(solution)/shard_map/all_to_all | solution.py:117
  81.7 1.8 convolution_convert_fusion.1
  83.5 1.9 reshape.160
  85.4 1.3 broadcast_in_dim.94
  86.6 53.4 %all_to_all.23 = bf16[16,12,4096]{2,1,0:T(8,128)(2,1)} all-to-all(bf16[16,12,4096]{2,1,0:T(8,128)(2,1)S(1)} %bitcast.82), channel_id=1, replica_groups=mesh['group'=2,'expert'=16] {'expert'}, dimensions={0} | all-to-all | bytes 3145728 | tf_op jit(solution)/shard_map/all_to_all | solution.py:146
  140.0 3.6 %reshape.162 = bf16[192,4096]{1,0:T(8,128)(2,1)} reshape(bf16[16,12,4096]{2,1,0:T(8,128)(2,1)} %all_to_all.23) | data formatting | bytes 3145728 | tf_op jit(solution)/shard_map/reshape | solution.py:148
  143.6 4.1 %fusion.5 = f32[192,384]{1,0:T(8,128)} fusion(bf16[192,4096]{1,0:T(8,128)(2,1)} %reshape.162, bf16[1,4096,384]{2,1,0:T(8,128)(2,1)} %param.29), kind=kOutput, calls=%fused_computation.12 | convolution fusion | flops 603979776 | bytes 5013504 | tf_op jit(solution)/shard_map/dot_general | solution.py:149
  147.6 5.4 %convolution_convert_fusion = bf16[192,4096]{1,0:T(8,128)(2,1)} fusion(bf16[1,384,4096]{2,1,0:T(8,128)(2,1)S(1)} %copy-done, bf16[192,4096]{1,0:T(8,128)(2,1)} %reshape.162, bf16[1,4096,384]{2,1,0:T(8,128)(2,1)} %param.30, f32[192,384]{1,0:T(8,128)} %fusion.5), kind=kOutput, calls=%fused_computation | convolution fusion | flops 1209188352 | bytes 9732096 | tf_op jit(solution)/shard_map/dot_general | solution.py:152
  153.1 3.4 %reshape.163 = bf16[16,12,4096]{2,1,0:T(8,128)(2,1)} reshape(bf16[192,4096]{1,0:T(8,128)(2,1)} %convolution_convert_fusion) | data formatting | bytes 3145728 | tf_op jit(solution)/shard_map/reshape | solution.py:153
  156.5 5.0 %all-to-all-start.2 = ((bf16[16,12,4096]{2,1,0:T(8,128)(2,1)}), bf16[16,12,4096]{2,1,0:T(8,128)(2,1)}, u32[]{:S(2)}, u32[]{:S(2)}) async-start(bf16[16,12,4096]{2,1,0:T(8,128)(2,1)} %reshape.163), calls=%async_computation.2 | async-start | bytes 4194304 | tf_op jit(solution)/shard_map/all_to_all | solution.py:154
  161.5 47.4 %all-to-all-done.2 = bf16[16,12,4096]{2,1,0:T(8,128)(2,1)} async-done(((bf16[16,12,4096]{2,1,0:T(8,128)(2,1)}), bf16[16,12,4096]{2,1,0:T(8,128)(2,1)}, u32[]{:S(2)}, u32[]{:S(2)}) %all-to-all-start.2) | async-done | bytes 1572896 | tf_op jit(solution)/shard_map/all_to_all | solution.py:154
  209.0 3.0 %convert_reduce_fusion = f32[4,12,4096]{2,1,0:T(8,128)} fusion(bf16[16,12,4096]{2,1,0:T(8,128)(2,1)} %all-to-all-done.2), kind=kLoop, calls=%fused_computation.4 | loop fusion | flops 1376256 | bytes 2359296 | tf_op jit(solution)/shard_map/reduce_sum | solution.py:155
  212.0 2.2 reshape.164
  214.2 2.3 %fusion = bf16[16,4096]{1,0:T(8,128)(2,1)} fusion(f32[48,16]{0,1:T(8,128)S(1)} %select_reduce_fusion, f32[48,4096]{1,0:T(8,128)} %reshape.164, f32[16,4096]{1,0:T(8,128)S(1)} %bitcast.85, bf16[16,4096]{1,0:T(8,128)(2,1)S(1)} %copy-done.2), kind=kOutput, calls=%fused_computation.3 | convolution fusion | flops 38010880 | bytes 1313792 | tf_op jit(solution)/shard_map/dot_general | solution.py:156
  (59 shorter events, 7.0 us)
Async XLA Ops:
  6.5 141.1 %copy-start = (bf16[1,384,4096]{2,1,0:T(8,128)(2,1)S(1)}, bf16[1,384,4096]{2,1,0:T(8,128)(2,1)}, u32[]{:S(2)}) copy-start(bf16[1,384,4096]{2,1,0:T(8,128)(2,1)} %param.31) | copy-start | bytes 9437188
  6.5 60.5 %all-gather.2.cloned.1.call-start = ((), (), s32[]{:S(2)}) async-start(), calls=%async_computation.3 | async-start | bytes 2228224 | tf_op jit(solution)/shard_map/all_gather | solution.py:113
  16.7 1.9 copy-start.1
  18.6 2.9 %copy-start.5 = (bf16[16,256]{1,0:T(8,128)(2,1)S(1)}, bf16[16,256]{1,0:T(8,128)(2,1)}, u32[]{:S(2)}) copy-start(bf16[16,256]{1,0:T(8,128)(2,1)} %param.18) | copy-start | bytes 24580
  21.5 4.3 %copy-start.7 = (s32[16,2]{0,1:T(2,128)S(1)}, s32[16,2]{0,1:T(2,128)}, u32[]{:S(2)}) copy-start(s32[16,2]{0,1:T(2,128)} %param.27) | copy-start | bytes 388
  21.5 5.0 %copy-start.6 = (bf16[4096]{0:T(1024)(128)(2,1)S(1)}, bf16[4096]{0:T(1024)(128)(2,1)}, u32[]{:S(2)}) copy-start(bf16[4096]{0:T(1024)(128)(2,1)} %param.26) | copy-start | bytes 24580
  25.1 56.5 %copy-start.2 = (bf16[16,4096]{1,0:T(8,128)(2,1)S(1)}, bf16[16,4096]{1,0:T(8,128)(2,1)}, u32[]{:S(2)}) copy-start(bf16[16,4096]{1,0:T(8,128)(2,1)} %param.24) | copy-start | bytes 393220
  70.6 10.9 %all-to-all-start = ((bf16[16,16,256]{2,1,0:T(8,128)(2,1)}), bf16[16,16,256]{2,1,0:T(8,128)(2,1)S(1)}, u32[]{:S(2)}, u32[]{:S(2)}) async-start(bf16[16,16,256]{2,1,0:T(8,128)(2,1)} %bitcast.9), calls=%async_computation | async-start | bytes 262144 | tf_op jit(solution)/shard_map/all_to_all | solution.py:117
  76.3 5.2 %copy-start.3 = (s32[16,2]{0,1:T(2,128)}, s32[16,2]{0,1:T(2,128)S(1)}, u32[]{:S(2)}) copy-start(s32[16,2]{0,1:T(2,128)S(1)} %multiply_add_fusion) | copy-start | bytes 388
  153.0 8.4 %copy-start.4 = (s32[16,2]{0,1:T(2,128)S(1)}, s32[16,2]{0,1:T(2,128)}, u32[]{:S(2)}) copy-start(s32[16,2]{0,1:T(2,128)} %copy-done.3) | copy-start | bytes 388
  153.1 8.4 %copy-start.8 = (f32[16,2]{0,1:T(2,128)S(1)}, f32[16,2]{0,1:T(2,128)}, u32[]{:S(2)}) copy-start(f32[16,2]{0,1:T(2,128)} %param.28) | copy-start | bytes 388
  156.5 52.5 %all-to-all-start.2 = ((bf16[16,12,4096]{2,1,0:T(8,128)(2,1)}), bf16[16,12,4096]{2,1,0:T(8,128)(2,1)}, u32[]{:S(2)}, u32[]{:S(2)}) async-start(bf16[16,12,4096]{2,1,0:T(8,128)(2,1)} %reshape.163), calls=%async_computation.2 | async-start | bytes 4194304 | tf_op jit(solution)/shard_map/all_to_all | solution.py:154
Sparse Core Ops, SparseCore 0:
  25.9 41.0 all-gather.1
where the time goes:
time: 224 us; the launch traced here: 223 us
  waiting for transfers between devices  92.5 us (41%)
  blocking collectives  53.4 us (24%)
  matrix products  23 us (10%)
  local copies, waits for them, and re-layouts  22.7 us (10%)
  between operations  13.6 us (6%)
  starting transfers between devices  10.7 us (5%)
  other arithmetic  7.5 us (3%)
    all_to_all x1, blocking collectives, per_device(): lax.all_to_all(outgoing, 'expert', split_axis=0, concat_axis=0, tiled=True)  53.4 us
    all_to_all x1, waiting for transfers between devices, per_device(): lax.all_to_all(partial_value, 'expert', split_axis=0, concat_axis=0, tile...  47.4 us
    all_gather x1, waiting for transfers between devices, per_device(): lax.all_gather(head_out, 'expert', axis=0, tiled=True)  40.5 us
    all_to_all x1, starting transfers between devices, per_device(): lax.all_to_all(spread, 'expert', split_axis=0, concat_axis=1, tiled=True)  5.7 us
    dot_general x1, matrix products, per_device(): jnp.dot(act, w_down[0], preferred_element_type=jnp.float32)  5.43 us
    all_to_all x1, starting transfers between devices, per_device(): lax.all_to_all(partial_value, 'expert', split_axis=0, concat_axis=0, tile...  4.95 us
    all_to_all x1, waiting for transfers between devices, per_device(): lax.all_to_all(spread, 'expert', split_axis=0, concat_axis=1, tiled=True)  4.48 us
  transfers between devices with their start and end apart: 3, of which 3 were waited for; matrix products, arithmetic and copies ran while one was open for 1% of the time, Pallas kernels for 0%

commit v1 on v0

--- a/solution.py
+++ b/solution.py
@@ -1,8 +1,11 @@
+import functools
 import math
 
 import jax
 import jax.numpy as jnp
 from jax import lax
+from jax.experimental import pallas as pl
+from jax.experimental.pallas import tpu as pltpu
 from jax.sharding import PartitionSpec as P
 
 D = 4096
@@ -79,6 +82,465 @@
         ..., None
     ] * fresh_value_rows.astype(jnp.float32).reshape(count_of_rows, KEY_VALUE_HEADS, 1, HEAD_SIZE)
     return mixed_output.reshape(count_of_rows, QUERY_HEADS * HEAD_SIZE).astype(jnp.bfloat16)
+
+
+MESH = pl.DeviceIdType.MESH
+LANES = 128
+
+
+def layer_kernel(
+    n,
+    chunks,
+    block_ref,
+    residual_ref,
+    gain_ref,
+    inverse_ref,
+    wo_hbm,
+    wg_hbm,
+    wu_hbm,
+    wd_hbm,
+    hidden_ref,
+    mixture_ref,
+    g1,
+    g2,
+    res,
+    wo,
+    wg,
+    wu,
+    wd,
+    gate,
+    upward,
+    squares,
+    act,
+    part,
+    from_core,
+    from_y,
+    from_z,
+    w_sem,
+    own_sem,
+    send1,
+    recv1,
+    send2,
+    recv2,
+    res_send,
+    res_recv,
+    core_send,
+    core_recv,
+    y_send,
+    y_recv,
+    z_send,
+    z_recv,
+):
+    levels = n // 4
+    rows = block_ref.shape[0]
+    total = n * rows
+    cols = residual_ref.shape[2]
+    width = D // chunks
+    me = lax.axis_index("expert")
+    z = lax.div(me, 4)
+    y = lax.rem(lax.div(me, 2), 2)
+    c = lax.rem(me, 2)
+    device = lambda zz, yy, cc: zz * 4 + yy * 2 + cc
+    beside_y = device(z, 1 - y, c)
+    beside_core = device(z, y, 1 - c)
+
+    weight_copies = [
+        pltpu.make_async_copy(source, target, w_sem.at[i])
+        for i, (source, target) in enumerate(
+            ((wo_hbm, wo), (wg_hbm, wg), (wu_hbm, wu), (wd_hbm, wd))
+        )
+    ]
+    for copy in weight_copies:
+        copy.start()
+
+    barrier = pltpu.get_barrier_semaphore()
+
+    @pl.loop(1, n)
+    def greet(k):
+        pl.semaphore_signal(
+            barrier, inc=1, device_id={"expert": lax.rem(me + k, n)}, device_id_type=MESH
+        )
+
+    own = pltpu.make_async_copy(block_ref, g1.at[z, y, c], own_sem.at[0])
+    own.start()
+    own.wait()
+    own_res = pltpu.make_async_copy(residual_ref.at[me], res.at[me], own_sem.at[1])
+    own_res.start()
+    own_res.wait()
+    pl.semaphore_wait(barrier, n - 1)
+
+    def gather(buf, send, recv, consume, after_first):
+        def copy(zz, yy, cc, way, target):
+            return pltpu.make_async_remote_copy(
+                src_ref=buf.at[zz, yy, cc],
+                dst_ref=buf.at[zz, yy, cc],
+                send_sem=send.at[way, zz, yy, cc],
+                recv_sem=recv.at[zz, yy, cc],
+                device_id={"expert": target},
+                device_id_type=MESH,
+            )
+
+        def up(zz):
+            return copy(zz, y, c, 0, device(jnp.minimum(z + 1, levels - 1), y, c))
+
+        def down(zz):
+            return copy(zz, y, c, 1, device(jnp.maximum(z - 1, 0), y, c))
+
+        def across(zz):
+            return copy(zz, y, c, 2, beside_y)
+
+        def beside(zz, yy):
+            return copy(zz, yy, c, 3, beside_core)
+
+        def landed(zz, yy, cc):
+            copy(zz, yy, cc, 3, beside_core).wait_recv()
+
+        def line(zz):
+            @pl.when(zz != z)
+            def _():
+                landed(zz, y, c)
+
+            @pl.when((zz <= z) & (z < levels - 1))
+            def _():
+                up(zz).start()
+
+            @pl.when((zz >= z) & (z > 0))
+            def _():
+                down(zz).start()
+
+            across(zz).start()
+            beside(zz, y).start()
+
+        def at_distance(distance, body):
+            @pl.loop(0, 2)
+            def _(sign):
+                zz = z - distance + 2 * distance * sign
+
+                @pl.when(
+                    (distance >= 0)
+                    & (zz >= 0)
+                    & (zz < levels)
+                    & ((distance > 0) | (sign == 0))
+                )
+                def _():
+                    body(zz)
+
+        def crossed(zz):
+            landed(zz, 1 - y, c)
+            beside(zz, 1 - y).start()
+
+        @pl.loop(0, levels + 2)
+        def step(s):
+            at_distance(s, line)
+            at_distance(s - 1, crossed)
+
+            @pl.when(s == 0)
+            def _():
+                after_first()
+
+            if consume is not None:
+                at_distance(s, lambda zz: consume(zz, y, c))
+                at_distance(s - 1, lambda zz: consume(zz, 1 - y, c))
+
+            def near(zz):
+                landed(zz, y, 1 - c)
+                if consume is not None:
+                    consume(zz, y, 1 - c)
+
+            def far(zz):
+                landed(zz, 1 - y, 1 - c)
+                if consume is not None:
+                    consume(zz, 1 - y, 1 - c)
+
+            at_distance(s - 1, near)
+            at_distance(s - 2, far)
+
+        def drain():
+            @pl.loop(0, levels)
+            def _(zz):
+                @pl.when((zz <= z) & (z < levels - 1))
+                def _():
+                    up(zz).wait_send()
+
+                @pl.when((zz >= z) & (z > 0))
+                def _():
+                    down(zz).wait_send()
+
+                across(zz).wait_send()
+                beside(zz, y).wait_send()
+                beside(zz, 1 - y).wait_send()
+
+        return drain
+
+    def residual_copy(k):
+        return pltpu.make_async_remote_copy(
+            src_ref=residual_ref.at[lax.rem(me + k, n)],
+            dst_ref=res.at[me],
+            send_sem=res_send.at[k],
+            recv_sem=res_recv.at[me],
+            device_id={"expert": lax.rem(me + k, n)},
+            device_id_type=MESH,
+        )
+
+    def residual_landed(k):
+        source = lax.rem(me + k, n)
+        pltpu.make_async_remote_copy(
+            src_ref=residual_ref.at[source],
+            dst_ref=res.at[source],
+            send_sem=res_send.at[k],
+            recv_sem=res_recv.at[source],
+            device_id={"expert": source},
+            device_id_type=MESH,
+        ).wait_recv()
+
+    def send_residual():
+        @pl.loop(1, n)
+        def _(k):
+            residual_copy(k).start()
+
+    drain1 = gather(g1, send1, recv1, None, send_residual)
+    weight_copies[0].wait()
+
+    @pl.loop(1, n)
+    def _(k):
+        residual_landed(k)
+
+    projected = jnp.zeros((total, cols), jnp.float32)
+    for k in range(0, D, 1024):
+        projected += jnp.dot(
+            g1[:, :, :, :, k : k + 1024].reshape(total, 1024),
+            wo[k : k + 1024, :],
+            preferred_element_type=jnp.float32,
+        )
+    hidden = res[...].reshape(total, cols).astype(jnp.float32) + projected.astype(
+        jnp.bfloat16
+    ).astype(jnp.float32)
+    g2[z, y, c] = (hidden * gain_ref[me]).astype(jnp.bfloat16)
+    gate[...] = jnp.zeros_like(gate)
+    upward[...] = jnp.zeros_like(upward)
+    squares[...] = jnp.zeros_like(squares)
+
+    def consume(zz, yy, cc):
+        d = device(zz, yy, cc)
+        block = g2[zz, yy, cc]
+        at = pl.ds(pl.multiple_of(d * cols, cols), cols)
+        gate[...] += jnp.dot(block, wg[at, :], preferred_element_type=jnp.float32)
+        upward[...] += jnp.dot(block, wu[at, :], preferred_element_type=jnp.float32)
+        plain = block.astype(jnp.float32) * inverse_ref[d]
+        squares[...] += jnp.sum(plain * plain, axis=1, keepdims=True)
+
+    def wait_weights():
+        weight_copies[1].wait()
+        weight_copies[2].wait()
+
+    drain2 = gather(g2, send2, recv2, consume, wait_weights)
+    hidden_ref[...] = g2[:, :, :, pl.ds(pl.multiple_of(me * rows, rows), rows), :].reshape(
+        n, rows, cols
+    )
+    scale = lax.rsqrt(squares[...] * (1.0 / D) + 1e-06)
+    gated = gate[...] * scale
+    act[...] = (gated / (1.0 + jnp.exp(-gated)) * (upward[...] * scale)).astype(jnp.bfloat16)
+    table = g1[:, :, :, :, D : D + LANES].reshape(total, LANES).astype(jnp.float32)
+    lane = lax.broadcasted_iota(jnp.int32, (total, LANES), 1)
+    table = jnp.where((lane < 3 * levels) & (lax.rem(lane, levels) == z), table, 0.0)
+    weight = jnp.sum(table, axis=1, keepdims=True)
+    weight_copies[3].wait()
+
+    def core_copy(j):
+        return pltpu.make_async_remote_copy(
+            src_ref=part.at[j, 1 - c],
+            dst_ref=from_core.at[j],
+            send_sem=core_send.at[j],
+            recv_sem=core_recv.at[j],
+            device_id={"expert": beside_core},
+            device_id_type=MESH,
+        )
+
+    def y_copy(j):
+        return pltpu.make_async_remote_copy(
+            src_ref=part.at[j, c, 1 - y],
+            dst_ref=from_y.at[j],
+            send_sem=y_send.at[j],
+            recv_sem=y_recv.at[j],
+            device_id={"expert": beside_y},
+            device_id_type=MESH,
+        )
+
+    def z_copy(j, goal, slot, target):
+        return pltpu.make_async_remote_copy(
+            src_ref=part.at[j, c, y, goal],
+            dst_ref=from_z.at[j, slot],
+            send_sem=z_send.at[j, goal],
+            recv_sem=z_recv.at[j, slot],
+            device_id={"expert": target},
+            device_id_type=MESH,
+        )
+
+    def z_landed(j, slot):
+        z_copy(j, 0, slot, beside_y).wait_recv()
+
+    def multiply(j):
+        value = jnp.dot(
+            act[...],
+            wd[:, pl.ds(pl.multiple_of(j * width, width), width)],
+            preferred_element_type=jnp.float32,
+        )
+        value = (value * weight).astype(jnp.bfloat16).reshape(levels, 2, 2, rows, width)
+        for yy in range(2):
+            for cc in range(2):
+                part[j, cc, yy] = value[:, yy, cc]
+        core_copy(j).start()
+
+    def add_core(j):
+        core_copy(j).wait_recv()
+        for yy in range(2):
+            part[j, c, yy] = (
+                part[j, c, yy].astype(jnp.float32) + from_core[j, yy].astype(jnp.float32)
+            ).astype(jnp.bfloat16)
+        y_copy(j).start()
+
+    def add_y(j):
+        y_copy(j).wait_recv()
+        part[j, c, y] = (
+            part[j, c, y].astype(jnp.float32) + from_y[j].astype(jnp.float32)
+        ).astype(jnp.bfloat16)
+
+    def chain(j, rising):
+        count = jnp.where(rising, levels - 1 - z, z)
+        first = jnp.where(rising, z == 0, z == levels - 1)
+        target = device(jnp.where(rising, z + 1, z - 1), y, c)
+
+        @pl.loop(0, count)
+        def _(k):
+            goal = jnp.where(rising, levels - 1 - k, k)
+
+            @pl.when(jnp.logical_not(first))
+            def _():
+                z_landed(j, goal)
+                part[j, c, y, goal] = (
+                    part[j, c, y, goal].astype(jnp.float32)
+                    + from_z[j, goal].astype(jnp.float32)
+                ).astype(jnp.bfloat16)
+
+            last_down = jnp.logical_not(rising) & (goal == z - 1)
+            z_copy(j, goal, jnp.where(last_down, levels, goal), target).start()
+
+    def chains(j):
+        rising = z < levels // 2
+        chain(j, rising)
+        chain(j, jnp.logical_not(rising))
+
+    def finish(j):
+        at = pl.ds(pl.multiple_of(j * width, width), width)
+        mixture_ref[:, at] = part[j, c, y, z].astype(jnp.float32)
+
+        @pl.when(z > 0)
+        def _():
+            z_landed(j, z)
+            mixture_ref[:, at] += from_z[j, z].astype(jnp.float32)
+
+        @pl.when(z < levels - 1)
+        def _():
+            z_landed(j, levels)
+            mixture_ref[:, at] += from_z[j, levels].astype(jnp.float32)
+
+    @pl.loop(0, chunks + 1)
+    def _(j):
+        @pl.when(j < chunks)
+        def _():
+            multiply(j)
+
+        @pl.when(j > 0)
+        def _():
+            add_core(j - 1)
+
+    @pl.loop(0, chunks)
+    def _(j):
+        add_y(j)
+        chains(j)
+
+    @pl.loop(0, chunks)
+    def _(j):
+        finish(j)
+
+    drain1()
+    drain2()
+
+    @pl.loop(1, n)
+    def _(k):
+        residual_copy(k).wait_send()
+
+    @pl.loop(0, chunks)
+    def _(j):
+        core_copy(j).wait_send()
+        y_copy(j).wait_send()
+
+        @pl.loop(0, levels)
+        def _(goal):
+            @pl.when(goal != z)
+            def _():
+                z_copy(j, goal, goal, beside_y).wait_send()
+
+
+def layer(n, block, residual, gain, inverse, wo, wg, wu, wd):
+    rows = block.shape[0]
+    total = n * rows
+    cols = residual.shape[2]
+    hidden_units = wg.shape[1]
+    levels = n // 4
+    chunks = max(4, levels)
+    width = D // chunks
+    bf16, f32 = jnp.bfloat16, jnp.float32
+    vmem = pl.BlockSpec(memory_space=pltpu.VMEM)
+    dma = pltpu.SemaphoreType.DMA
+    return pl.pallas_call(
+        functools.partial(layer_kernel, n, chunks),
+        out_shape=(
+            jax.ShapeDtypeStruct((n, rows, cols), bf16),
+            jax.ShapeDtypeStruct((rows, D), f32),
+        ),
+        in_specs=[vmem] * 4 + [pl.BlockSpec(memory_space=pl.ANY)] * 4,
+        out_specs=(vmem, vmem),
+        scratch_shapes=[
+            pltpu.VMEM((levels, 2, 2, rows, D + LANES), bf16),
+            pltpu.VMEM((levels, 2, 2, total, cols), bf16),
+            pltpu.VMEM((n, rows, cols), bf16),
+            pltpu.VMEM(wo.shape, bf16),
+            pltpu.VMEM(wg.shape, bf16),
+            pltpu.VMEM(wu.shape, bf16),
+            pltpu.VMEM(wd.shape, bf16),
+            pltpu.VMEM((total, hidden_units), f32),
+            pltpu.VMEM((total, hidden_units), f32),
+            pltpu.VMEM((total, 1), f32),
+            pltpu.VMEM((total, hidden_units), bf16),
+            pltpu.VMEM((chunks, 2, 2, levels, rows, width), bf16),
+            pltpu.VMEM((chunks, 2, levels, rows, width), bf16),
+            pltpu.VMEM((chunks, levels, rows, width), bf16),
+            pltpu.VMEM((chunks, levels + 1, rows, width), bf16),
+            dma((4,)),
+            dma((2,)),
+            dma((4, levels, 2, 2)),
+            dma((levels, 2, 2)),
+            dma((4, levels, 2, 2)),
+            dma((levels, 2, 2)),
+            dma((n,)),
+            dma((n,)),
+            dma((chunks,)),
+            dma((chunks,)),
+            dma((chunks,)),
+            dma((chunks,)),
+            dma((chunks, levels)),
+            dma((chunks, levels + 1)),
+        ],
+        compiler_params=pltpu.CompilerParams(
+            collective_id=0, has_side_effects=True, vmem_limit_bytes=62 * 1024 * 1024
+        ),
+        cost_estimate=pl.CostEstimate(
+            flops=2 * total * D * (cols + 3 * hidden_units),
+            bytes_accessed=2 * D * (cols + 3 * hidden_units),
+            transcendentals=total * hidden_units,
+        ),
+    )(block, residual, gain, inverse, wo, wg, wu, wd)
 
 
 def per_device(
@@ -109,56 +571,34 @@
         last_page_fill,
         local_page_ranking[0],
     )
-    spread = jnp.dot(
-        lax.all_gather(head_out, "expert", axis=0, tiled=True),
+    n = lax.axis_size("expert")
+    experts = n // SHARDS
+    rows = head_out.shape[0]
+    cols = out_weight.shape[1]
+    ids = jnp.arange(experts, dtype=jnp.int32)
+    table = jnp.sum(
+        jnp.where(routes[:, :, None] == ids[None, None, :], route_weight[:, :, None], 0.0), axis=1
+    )
+    high = lax.reduce_precision(table, 8, 7)
+    middle = lax.reduce_precision(table - high, 8, 7)
+    low = table - high - middle
+    packed = jnp.concatenate([high, middle, low], axis=1).astype(jnp.bfloat16)
+    packed = jnp.pad(packed, ((0, 0), (0, LANES - 3 * experts)))
+    block = jnp.concatenate([head_out, packed], axis=1)
+    gain = norm_gain.astype(jnp.float32)
+    inverse = 1.0 / gain
+    scaled, mixture = layer(
+        n,
+        block,
+        residual.reshape(rows, n, cols).transpose(1, 0, 2),
+        gain.reshape(n, 1, cols),
+        inverse.reshape(n, 1, cols),
         out_weight,
-        preferred_element_type=jnp.float32,
-    ).astype(jnp.bfloat16)
-    projected = lax.all_to_all(spread, "expert", split_axis=0, concat_axis=1, tiled=True)
-    hidden = residual.astype(jnp.float32) + projected.astype(jnp.float32)
-    normed = (
-        hidden
-        * lax.rsqrt(jnp.mean(hidden * hidden, axis=-1, keepdims=True) + 1e-06)
-        * norm_gain.astype(jnp.float32)
-    ).astype(jnp.bfloat16)
-    device_list = lax.axis_size("expert")
-    experts = device_list // SHARDS
-    count_of_rows = normed.shape[0]
-    top_count = routes.shape[1]
-    flat_routes = routes.reshape(-1)
-    onehot = (flat_routes[:, None] == jnp.arange(experts, dtype=jnp.int32)[None, :]).astype(
-        jnp.int32
-    )
-    counts = jnp.cumsum(onehot, axis=0)
-    slot_index = jnp.sum(onehot * (counts - 1), axis=1)
-    place_index = flat_routes * CAP + slot_index
-    chosen = (jnp.arange(experts * CAP, dtype=jnp.int32)[:, None] == place_index[None, :]).reshape(
-        experts * CAP, count_of_rows, top_count
-    )
-    picked = jnp.any(chosen, axis=2).astype(jnp.bfloat16)
-    weighted = jnp.sum(jnp.where(chosen, route_weight[None, :, :], 0.0), axis=2)
-    buffer = (
-        jnp.dot(picked, normed, preferred_element_type=jnp.float32)
-        .astype(jnp.bfloat16)
-        .reshape(experts, CAP, D)
-    )
-    outgoing = jnp.repeat(buffer, SHARDS, axis=0)
-    arrived = lax.all_to_all(outgoing, "expert", split_axis=0, concat_axis=0, tiled=True)
-    item_count = arrived.shape[1]
-    rows_in = arrived.reshape(-1, D)
-    gate = jnp.dot(rows_in, w_gate[0], preferred_element_type=jnp.float32)
-    upward = jnp.dot(rows_in, w_up[0], preferred_element_type=jnp.float32)
-    act = (jax.nn.silu(gate) * upward).astype(jnp.bfloat16)
-    output = jnp.dot(act, w_down[0], preferred_element_type=jnp.float32).astype(jnp.bfloat16)
-    partial_value = output.reshape(arrived.shape[0], item_count, D)
-    returned = lax.all_to_all(partial_value, "expert", split_axis=0, concat_axis=0, tiled=True)
-    summed = jnp.sum(returned.reshape(experts, SHARDS, CAP, D).astype(jnp.float32), axis=1)
-    mixture = jnp.dot(
-        weighted.T,
-        summed.reshape(experts * CAP, D),
-        precision=lax.Precision.HIGHEST,
-        preferred_element_type=jnp.float32,
-    )
+        w_gate[0],
+        w_up[0],
+        w_down[0],
+    )
+    hidden = scaled.transpose(1, 0, 2).reshape(rows, D).astype(jnp.float32) * inverse
     return (hidden + mixture).astype(jnp.bfloat16)
 
 

time: 224 us -> 96.7 us (0.43)
  the two profiles are of different devices: /device:TPU:13 before, /device:TPU:0 now
where the time goes in v1:
time: 96.7 us; the launch traced here: 96.4 us
  Pallas kernels  75.1 us (78%)
  other arithmetic  9.97 us (10%)
  matrix products  6.26 us (6%)
  local copies, waits for them, and re-layouts  4.83 us (5%)
    pallas_call x1, Pallas kernels, layer(): pl.pallas_call(functools.partial(layer_kernel, n, chunks), out_shape=(jax...  75.1 us
    dot_general x1, matrix products, local_attention(): jnp.einsum('rhgt,thd->rhgd', weights, value_matrix, preferred_element_typ...  3.27 us
    reduce_sum x1, other arithmetic, local_attention(): denominator = jnp.sum(raised, axis=-1) + own_raised  2.87 us
    dot_general x1, matrix products, local_attention(): jnp.einsum('rhgd,thd->rhgt', query_head_rows, key_matrix, preferred_eleme...  2.82 us

profile of v1, /device:TPU:0, one launch (start us, length us, event | category | flops | bytes accessed | tf_op | source)
XLA Modules:
  0.0 96.4 jit_solution(6990848293716192485)
XLA Ops:
  0.0 0.7 copy.46
  0.8 0.1 reduce
  0.9 0.7 fusion.18
  1.5 0.1 select_reduce_fusion.2
  1.6 0.8 select_reduce_fusion
  2.4 0.1 and.18
  2.6 0.2 and.19
  2.8 0.1 broadcast_reduce_fusion
  3.0 0.7 bitcast_add_fusion
  3.7 0.1 compare_and_fusion
  3.8 0.9 copy.68
  4.8 1.3 %reshape.119 = bf16[2048,2,128]{2,1,0:T(2,128)(2,1)S(1)} reshape(bf16[32,64,256]{2,1,0:T(8,128)(2,1)} %param.19) | data formatting | bytes 2097152 | tf_op jit(solution)/shard_map/reshape | solution.py:54
  6.1 2.8 %fusion.19 = (f32[16,2,16]{2,0,1:T(8,128)S(1)}, f32[16,2,16,2048]{3,2,0,1:T(8,128)}) fusion(bf16[16,2,16,128]{3,2,1,0:T(8,128)(2,1)S(1)} %bitcast.79, bf16[2048,2,128,1]{2,1,0,3:T(2,128)(2,1)S(1)} %bitcast.71, pred[16,2048]{1,0:T(8,128)(4,1)S(1)} %compare_and_fusion), kind=kOutput, calls=%fused_computation.52 | convolution fusion | flops 271580672 | bytes 5408768 | tf_op jit(solution)/shard_map/rhgd,thd->rhgt/dot_general | solution.py:57
  9.0 0.2 fusion.20
  9.1 2.9 %fusion = f32[16,2,16]{2,0,1:T(8,128)S(1)} fusion(f32[16,2,16,2048]{3,2,0,1:T(8,128)} %get-tuple-element.19, f32[16,2,16]{2,0,1:T(8,128)S(1)} %fusion.8), kind=kLoop, calls=%fused_computation.3 | loop fusion | flops 2096640 | bytes 4198400 | tf_op jit(solution)/shard_map/reduce_sum | solution.py:75
  12.1 0.3 reshape.122
  12.4 3.3 %fusion.4 = bf16[16,2,16,128]{3,2,0,1:T(8,128)(2,1)S(1)} fusion(f32[16,2,16,2048]{3,2,0,1:T(8,128)} %get-tuple-element.19, f32[16,2,16]{2,0,1:T(8,128)S(1)} %get-tuple-element.14, f32[16,2,16]{2,0,1:T(8,128)S(1)} %fusion.8, bf16[2048,2,128,1]{2,1,0,3:T(2,128)(2,1)S(1)} %bitcast.70, f32[16,2,128]{2,0,1:T(8,128)S(1)} %copy_bitcast_fusion.1, ...), kind=kOutput, calls=%fused_computation.7 | convolution fusion | flops 271777792 | bytes 5396480 | tf_op jit(solution)/shard_map/rhgt,thd->rhgd/dot_general | solution.py:78
  16.1 0.7 pad_maximum_fusion.block_ref
  16.8 0.6 broadcast_divide_fusion
  17.4 0.7 copy.99
  18.0 0.6 convert_element_type.39
  18.7 75.1 %shard_map.154 = (bf16[16,16,256]{2,1,0:T(8,128)(2,1)}, f32[16,4096]{1,0:T(8,128)}) custom-call(bf16[16,4224]{1,0:T(8,128)(2,1)} %pad_maximum_fusion.block_ref, bf16[16,16,256]{2,1,0:T(8,128)(2,1)} %bitcast.73, f32[16,1,256]{2,1,0:T(1,128)} %bitcast.81, f32[16,1,256]{2,1,0:T(1,128)} %bitcast.76, bf16[4096,256]{1,0:T(8,128)(2,1)} %wo_hbm.1, ...), custom_call_target="tpu_custom_call" | custom-call | flops 2952790016 | bytes 11534336 | tf_op jit(solution)/shard_map/pallas_call | solution.py:496
  93.8 0.9 convert_bitcast_fusion
  94.7 1.6 %add_convert_fusion = bf16[16,4096]{1,0:T(8,128)(2,1)} fusion(f32[16,4096]{1,0:T(8,128)} %get-tuple-element.8, f32[16,4096]{1,0:T(8,128)S(1)} %bitcast.72, f32[4096]{0:T(1024)S(1)} %copy-done.1), kind=kLoop, calls=%fused_computation.11 | loop fusion | flops 196608 | bytes 671744 | tf_op jit(solution)/shard_map/convert_element_type | solution.py:602
  (37 shorter events, 0.7 us)
Async XLA Ops:
  4.7 4.2 %copy-start.4 = (bf16[16,256]{1,0:T(8,128)(2,1)S(1)}, bf16[16,256]{1,0:T(8,128)(2,1)}, u32[]{:S(2)}) copy-start(bf16[16,256]{1,0:T(8,128)(2,1)} %param.17) | copy-start | bytes 24580
  6.1 6.0 %copy-start = (bf16[32,64,256]{2,1,0:T(8,128)(2,1)S(1)}, bf16[32,64,256]{2,1,0:T(8,128)(2,1)}, u32[]{:S(2)}) copy-start(bf16[32,64,256]{2,1,0:T(8,128)(2,1)} %param.20) | copy-start | bytes 3145732
  8.9 3.4 %copy-start.5 = (bf16[16,256]{1,0:T(8,128)(2,1)S(1)}, bf16[16,256]{1,0:T(8,128)(2,1)}, u32[]{:S(2)}) copy-start(bf16[16,256]{1,0:T(8,128)(2,1)} %param.18) | copy-start | bytes 24580
  12.4 3.4 %copy-start.6 = (f32[16,2]{0,1:T(2,128)S(1)}, f32[16,2]{0,1:T(2,128)}, u32[]{:S(2)}) copy-start(f32[16,2]{0,1:T(2,128)} %param.28) | copy-start | bytes 388
  12.4 3.4 %copy-start.7 = (s32[16,2]{0,1:T(2,128)S(1)}, s32[16,2]{0,1:T(2,128)}, u32[]{:S(2)}) copy-start(s32[16,2]{0,1:T(2,128)} %param.27) | copy-start | bytes 388
  12.4 4.4 %copy-start.3 = (bf16[4096]{0:T(1024)(128)(2,1)S(1)}, bf16[4096]{0:T(1024)(128)(2,1)}, u32[]{:S(2)}) copy-start(bf16[4096]{0:T(1024)(128)(2,1)} %param.26) | copy-start | bytes 24580
  12.4 5.0 %copy-start.2 = (bf16[16,4096]{1,0:T(8,128)(2,1)S(1)}, bf16[16,4096]{1,0:T(8,128)(2,1)}, u32[]{:S(2)}) copy-start(bf16[16,4096]{1,0:T(8,128)(2,1)} %param.24) | copy-start | bytes 393220
  18.7 76.1 %copy-start.1 = (f32[4096]{0:T(1024)S(1)}, f32[4096]{0:T(1024)}, u32[]{:S(2)}) copy-start(f32[4096]{0:T(1024)} %broadcast_divide_fusion) | copy-start | bytes 49156

commit v2 on v1

--- a/solution.py
+++ b/solution.py
@@ -12,95 +12,126 @@
 QUERY_HEADS = 32
 KEY_VALUE_HEADS = 2
 HEAD_SIZE = 128
-SHARDS = 4
-CAP = 12
-
-
-def local_attention(
-    queries,
-    fresh_key_rows,
-    fresh_value_rows,
-    key_cache_pages,
-    value_cache_pages,
-    sequence_page_table,
-    last_page_fill,
-    local_page_ranking,
-):
-    count_of_rows = queries.shape[0]
-    pooled_pages = local_page_ranking.shape[0]
-    page_length = key_cache_pages.shape[1]
-    query_group_width = QUERY_HEADS // KEY_VALUE_HEADS
-    first_page = jnp.cumsum(sequence_page_table) - sequence_page_table
-    page_slot = jnp.arange(pooled_pages, dtype=jnp.int32)
-    row_ids = jnp.arange(count_of_rows, dtype=jnp.int32)
-    inside = (page_slot[:, None] >= first_page[None, :]) & (
-        page_slot[:, None] < (first_page + sequence_page_table)[None, :]
-    )
-    owner_slot = jnp.sum(jnp.where(inside, row_ids[None, :], 0), axis=1)
-    index_slot = page_slot - jnp.sum(jnp.where(inside, first_page[None, :], 0), axis=1)
-    placed = local_page_ranking[None, :] == page_slot[:, None]
-    page_owner = jnp.sum(jnp.where(placed, owner_slot[None, :], 0), axis=1)
-    page_index = jnp.sum(jnp.where(placed, index_slot[None, :], 0), axis=1)
-    cached = (sequence_page_table - 1) * page_length + last_page_fill
-    token_place = (
-        page_index[:, None] * page_length + jnp.arange(page_length, dtype=jnp.int32)[None, :]
-    )
-    visible = (page_owner[None, :, None] == row_ids[:, None, None]) & (
-        token_place[None, :, :] < cached[:, None, None]
-    )
-    visible = visible.reshape(count_of_rows, pooled_pages * page_length)
-    score_scale = 1.0 / math.sqrt(HEAD_SIZE)
-    query_head_rows = queries.reshape(count_of_rows, KEY_VALUE_HEADS, query_group_width, HEAD_SIZE)
-    key_matrix = key_cache_pages.reshape(pooled_pages * page_length, KEY_VALUE_HEADS, HEAD_SIZE)
-    value_matrix = value_cache_pages.reshape(pooled_pages * page_length, KEY_VALUE_HEADS, HEAD_SIZE)
-    scores = (
-        jnp.einsum(
-            "rhgd,thd->rhgt", query_head_rows, key_matrix, preferred_element_type=jnp.float32
-        )
-        * score_scale
-    )
-    self_score = (
-        jnp.einsum(
-            "jqnu,jqu->jqn",
-            query_head_rows,
-            fresh_key_rows.reshape(count_of_rows, KEY_VALUE_HEADS, HEAD_SIZE),
-            preferred_element_type=jnp.float32,
-        )
-        * score_scale
-    )
-    scores = jnp.where(visible[:, None, None, :], scores, -jnp.inf)
-    highest = jnp.maximum(jnp.max(scores, axis=-1), self_score)
-    raised = jnp.exp(scores - highest[..., None])
-    own_raised = jnp.exp(self_score - highest)
-    denominator = jnp.sum(raised, axis=-1) + own_raised
-    weights = (raised / denominator[..., None]).astype(jnp.bfloat16)
-    self_weight = (own_raised / denominator).astype(jnp.bfloat16)
-    mixed_output = jnp.einsum(
-        "rhgt,thd->rhgd", weights, value_matrix, preferred_element_type=jnp.float32
-    )
-    mixed_output = mixed_output + self_weight.astype(jnp.float32)[
-        ..., None
-    ] * fresh_value_rows.astype(jnp.float32).reshape(count_of_rows, KEY_VALUE_HEADS, 1, HEAD_SIZE)
-    return mixed_output.reshape(count_of_rows, QUERY_HEADS * HEAD_SIZE).astype(jnp.bfloat16)
 
 
 MESH = pl.DeviceIdType.MESH
 LANES = 128
+
+
+def packed_routes(levels, rows, routes_ref, route_weight_ref):
+    lane = lax.broadcasted_iota(jnp.int32, (rows, LANES), 1)
+    expert = lax.rem(lane, levels)
+    table = jnp.zeros((rows, LANES), jnp.float32)
+    for t in range(routes_ref.shape[1]):
+        table += jnp.where(
+            routes_ref[:, t : t + 1] == expert, route_weight_ref[:, t : t + 1], 0.0
+        )
+    high = table.astype(jnp.bfloat16).astype(jnp.float32)
+    middle = (table - high).astype(jnp.bfloat16).astype(jnp.float32)
+    low = table - high - middle
+    piece = jnp.where(lane < levels, high, jnp.where(lane < 2 * levels, middle, low))
+    return jnp.where(lane < 3 * levels, piece, 0.0).astype(jnp.bfloat16)
+
+
+def attend(
+    query_ref,
+    fresh_key_ref,
+    fresh_value_ref,
+    count_ref,
+    fill_ref,
+    ranking_ref,
+    keys,
+    values,
+    by_head,
+    out,
+):
+    f32 = jnp.float32
+    rows = query_ref.shape[0]
+    pages, page, _ = keys.shape
+    tokens = pages * page
+    heads = QUERY_HEADS // KEY_VALUE_HEADS
+    group = heads * rows
+    iota = lambda shape, axis: lax.broadcasted_iota(jnp.int32, shape, axis)
+    diagonal = iota((pages, pages), 0) == iota((pages, pages), 1)
+    page_of_slot = jnp.sum(
+        jnp.where(diagonal, ranking_ref[...].astype(f32), 0.0), axis=1, keepdims=True
+    )
+    token = iota((pages, tokens), 1)
+    page_of_token = lax.div(token, page).astype(f32)
+    slot = jnp.sum(
+        jnp.where(page_of_token == page_of_slot, iota((pages, tokens), 0).astype(f32), 0.0),
+        axis=0,
+        keepdims=True,
+    )
+    place = slot * page + lax.rem(token[:1], page).astype(f32)
+    below = iota((rows, rows), 1) < iota((rows, rows), 0)
+    same = iota((rows, rows), 1) == iota((rows, rows), 0)
+    counts = count_ref[...].astype(f32)
+    lengths = (counts - 1.0) * page + fill_ref[...].astype(f32)
+    first = page * jnp.sum(jnp.where(below, counts, 0.0), axis=1, keepdims=True)
+    last = first + jnp.sum(jnp.where(same, lengths, 0.0), axis=1, keepdims=True)
+    visible = (place >= first) & (place < last)
+    bias = jnp.where(visible, 0.0, -jnp.inf)
+    scale = 1.0 / math.sqrt(HEAD_SIZE)
+    for g in range(KEY_VALUE_HEADS):
+        features = slice(g * HEAD_SIZE, (g + 1) * HEAD_SIZE)
+        for h in range(heads):
+            at = (g * heads + h) * HEAD_SIZE
+            by_head[h] = query_ref[:, at : at + HEAD_SIZE]
+        query = by_head[...]
+        fresh_key = fresh_key_ref[:, features].astype(f32)
+        fresh_value = fresh_value_ref[:, features].astype(f32)
+        own = scale * jnp.sum(query.astype(f32) * fresh_key[None], axis=2, keepdims=True)
+        scores = lax.dot_general(
+            query.reshape(group, HEAD_SIZE),
+            keys[:, :, features].reshape(tokens, HEAD_SIZE),
+            (((1,), (1,)), ((), ())),
+            preferred_element_type=f32,
+        )
+        scores = scores.reshape(heads, rows, tokens) * scale + bias[None]
+        highest = jnp.maximum(jnp.max(scores, axis=2, keepdims=True), own)
+        raised = jnp.exp(scores - highest)
+        own_raised = jnp.exp(own - highest)
+        inverse = 1.0 / (jnp.sum(raised, axis=2, keepdims=True) + own_raised)
+        mixed = jnp.dot(
+            raised.astype(jnp.bfloat16).reshape(group, tokens),
+            values[:, :, features].reshape(tokens, HEAD_SIZE),
+            preferred_element_type=f32,
+        )
+        mixed = mixed.reshape(heads, rows, HEAD_SIZE) + own_raised * fresh_value[None]
+        mixed = (mixed * inverse).astype(jnp.bfloat16)
+        for h in range(heads):
+            at = (g * heads + h) * HEAD_SIZE
+            out[:, at : at + HEAD_SIZE] = mixed[h]
 
 
 def layer_kernel(
     n,
     chunks,
-    block_ref,
+    query_ref,
+    fresh_key_ref,
+    fresh_value_ref,
+    count_ref,
+    fill_ref,
+    ranking_ref,
     residual_ref,
     gain_ref,
-    inverse_ref,
+    routes_ref,
+    route_weight_ref,
+    key_hbm,
+    value_hbm,
     wo_hbm,
     wg_hbm,
     wu_hbm,
     wd_hbm,
-    hidden_ref,
-    mixture_ref,
+    out_ref,
+    keys,
+    values,
+    by_head,
+    residual_out,
+    gains,
+    inverse,
+    hidden_own,
     g1,
     g2,
     res,
@@ -117,7 +148,6 @@
     from_y,
     from_z,
     w_sem,
-    own_sem,
     send1,
     recv1,
     send2,
@@ -132,9 +162,9 @@
     z_recv,
 ):
     levels = n // 4
-    rows = block_ref.shape[0]
+    rows = query_ref.shape[0]
     total = n * rows
-    cols = residual_ref.shape[2]
+    cols = D // n
     width = D // chunks
     me = lax.axis_index("expert")
     z = lax.div(me, 4)
@@ -144,6 +174,12 @@
     beside_y = device(z, 1 - y, c)
     beside_core = device(z, y, 1 - c)
 
+    cache_copies = [
+        pltpu.make_async_copy(key_hbm, keys, w_sem.at[4]),
+        pltpu.make_async_copy(value_hbm, values, w_sem.at[5]),
+    ]
+    for copy in cache_copies:
+        copy.start()
     weight_copies = [
         pltpu.make_async_copy(source, target, w_sem.at[i])
         for i, (source, target) in enumerate(
@@ -161,12 +197,27 @@
             barrier, inc=1, device_id={"expert": lax.rem(me + k, n)}, device_id_type=MESH
         )
 
-    own = pltpu.make_async_copy(block_ref, g1.at[z, y, c], own_sem.at[0])
-    own.start()
-    own.wait()
-    own_res = pltpu.make_async_copy(residual_ref.at[me], res.at[me], own_sem.at[1])
-    own_res.start()
-    own_res.wait()
+    for d in range(n):
+        at = slice(d * cols, (d + 1) * cols)
+        residual_out[d] = residual_ref[:, at]
+        gains[d] = gain_ref[:, at].astype(jnp.float32)
+        inverse[d] = 1.0 / gains[d]
+    res[me] = residual_out[me]
+    g1[z, y, c, :, D:] = packed_routes(levels, rows, routes_ref, route_weight_ref)
+    for copy in cache_copies:
+        copy.wait()
+    attend(
+        query_ref,
+        fresh_key_ref,
+        fresh_value_ref,
+        count_ref,
+        fill_ref,
+        ranking_ref,
+        keys,
+        values,
+        by_head,
+        g1.at[z, y, c],
+    )
     pl.semaphore_wait(barrier, n - 1)
 
     def gather(buf, send, recv, consume, after_first):
@@ -274,7 +325,7 @@
 
     def residual_copy(k):
         return pltpu.make_async_remote_copy(
-            src_ref=residual_ref.at[lax.rem(me + k, n)],
+            src_ref=residual_out.at[lax.rem(me + k, n)],
             dst_ref=res.at[me],
             send_sem=res_send.at[k],
             recv_sem=res_recv.at[me],
@@ -285,7 +336,7 @@
     def residual_landed(k):
         source = lax.rem(me + k, n)
         pltpu.make_async_remote_copy(
-            src_ref=residual_ref.at[source],
+            src_ref=residual_out.at[source],
             dst_ref=res.at[source],
             send_sem=res_send.at[k],
             recv_sem=res_recv.at[source],
@@ -315,7 +366,7 @@
     hidden = res[...].reshape(total, cols).astype(jnp.float32) + projected.astype(
         jnp.bfloat16
     ).astype(jnp.float32)
-    g2[z, y, c] = (hidden * gain_ref[me]).astype(jnp.bfloat16)
+    g2[z, y, c] = (hidden * gains[me]).astype(jnp.bfloat16)
     gate[...] = jnp.zeros_like(gate)
     upward[...] = jnp.zeros_like(upward)
     squares[...] = jnp.zeros_like(squares)
@@ -326,7 +377,7 @@
         at = pl.ds(pl.multiple_of(d * cols, cols), cols)
         gate[...] += jnp.dot(block, wg[at, :], preferred_element_type=jnp.float32)
         upward[...] += jnp.dot(block, wu[at, :], preferred_element_type=jnp.float32)
-        plain = block.astype(jnp.float32) * inverse_ref[d]
+        plain = block.astype(jnp.float32) * inverse[d]
         squares[...] += jnp.sum(plain * plain, axis=1, keepdims=True)
 
     def wait_weights():
@@ -334,9 +385,6 @@
         weight_copies[2].wait()
 
     drain2 = gather(g2, send2, recv2, consume, wait_weights)
-    hidden_ref[...] = g2[:, :, :, pl.ds(pl.multiple_of(me * rows, rows), rows), :].reshape(
-        n, rows, cols
-    )
     scale = lax.rsqrt(squares[...] * (1.0 / D) + 1e-06)
     gated = gate[...] * scale
     act[...] = (gated / (1.0 + jnp.exp(-gated)) * (upward[...] * scale)).astype(jnp.bfloat16)
@@ -432,17 +480,19 @@
 
     def finish(j):
         at = pl.ds(pl.multiple_of(j * width, width), width)
-        mixture_ref[:, at] = part[j, c, y, z].astype(jnp.float32)
+        hidden_own[:, at] += part[j, c, y, z].astype(jnp.float32)
 
         @pl.when(z > 0)
         def _():
             z_landed(j, z)
-            mixture_ref[:, at] += from_z[j, z].astype(jnp.float32)
+            hidden_own[:, at] += from_z[j, z].astype(jnp.float32)
 
         @pl.when(z < levels - 1)
         def _():
             z_landed(j, levels)
-            mixture_ref[:, at] += from_z[j, levels].astype(jnp.float32)
+            hidden_own[:, at] += from_z[j, levels].astype(jnp.float32)
+
+        out_ref[:, at] = hidden_own[:, at].astype(jnp.bfloat16)
 
     @pl.loop(0, chunks + 1)
     def _(j):
@@ -454,6 +504,10 @@
         def _():
             add_core(j - 1)
 
+    for d in range(n):
+        mine = g2[d // 4, d // 2 % 2, d % 2, pl.ds(pl.multiple_of(me * rows, rows), rows), :]
+        hidden_own[:, d * cols : (d + 1) * cols] = mine.astype(jnp.float32) * inverse[d]
+
     @pl.loop(0, chunks)
     def _(j):
         add_y(j)
@@ -482,10 +536,11 @@
                 z_copy(j, goal, goal, beside_y).wait_send()
 
 
-def layer(n, block, residual, gain, inverse, wo, wg, wu, wd):
-    rows = block.shape[0]
+def layer(n, *operands):
+    queries, keys, wo, wg, wu, wd = operands[0], operands[10], *operands[12:]
+    rows = queries.shape[0]
     total = n * rows
-    cols = residual.shape[2]
+    cols = wo.shape[1]
     hidden_units = wg.shape[1]
     levels = n // 4
     chunks = max(4, levels)
@@ -495,13 +550,17 @@
     dma = pltpu.SemaphoreType.DMA
     return pl.pallas_call(
         functools.partial(layer_kernel, n, chunks),
-        out_shape=(
-            jax.ShapeDtypeStruct((n, rows, cols), bf16),
-            jax.ShapeDtypeStruct((rows, D), f32),
-        ),
-        in_specs=[vmem] * 4 + [pl.BlockSpec(memory_space=pl.ANY)] * 4,
-        out_specs=(vmem, vmem),
+        out_shape=jax.ShapeDtypeStruct((rows, D), bf16),
+        in_specs=[vmem] * 10 + [pl.BlockSpec(memory_space=pl.ANY)] * 6,
+        out_specs=vmem,
         scratch_shapes=[
+            pltpu.VMEM(keys.shape, bf16),
+            pltpu.VMEM(keys.shape, bf16),
+            pltpu.VMEM((QUERY_HEADS // KEY_VALUE_HEADS, rows, HEAD_SIZE), bf16),
+            pltpu.VMEM((n, rows, cols), bf16),
+            pltpu.VMEM((n, 1, cols), f32),
+            pltpu.VMEM((n, 1, cols), f32),
+            pltpu.VMEM((rows, D), f32),
             pltpu.VMEM((levels, 2, 2, rows, D + LANES), bf16),
             pltpu.VMEM((levels, 2, 2, total, cols), bf16),
             pltpu.VMEM((n, rows, cols), bf16),
@@ -517,8 +576,7 @@
             pltpu.VMEM((chunks, 2, levels, rows, width), bf16),
             pltpu.VMEM((chunks, levels, rows, width), bf16),
             pltpu.VMEM((chunks, levels + 1, rows, width), bf16),
-            dma((4,)),
-            dma((2,)),
+            dma((6,)),
             dma((4, levels, 2, 2)),
             dma((levels, 2, 2)),
             dma((4, levels, 2, 2)),
@@ -540,7 +598,7 @@
             bytes_accessed=2 * D * (cols + 3 * hidden_units),
             transcendentals=total * hidden_units,
         ),
-    )(block, residual, gain, inverse, wo, wg, wu, wd)
+    )(*operands)
 
 
 def per_device(
@@ -561,45 +619,25 @@
     w_up,
     w_down,
 ):
-    head_out = local_attention(
+    return layer(
+        lax.axis_size("expert"),
         queries,
         fresh_key_rows,
         fresh_value_rows,
+        sequence_page_table,
+        last_page_fill.reshape(1, -1),
+        local_page_ranking,
+        residual,
+        norm_gain.reshape(1, -1),
+        routes,
+        route_weight,
         key_cache_pages,
         value_cache_pages,
-        sequence_page_table[0],
-        last_page_fill,
-        local_page_ranking[0],
-    )
-    n = lax.axis_size("expert")
-    experts = n // SHARDS
-    rows = head_out.shape[0]
-    cols = out_weight.shape[1]
-    ids = jnp.arange(experts, dtype=jnp.int32)
-    table = jnp.sum(
-        jnp.where(routes[:, :, None] == ids[None, None, :], route_weight[:, :, None], 0.0), axis=1
-    )
-    high = lax.reduce_precision(table, 8, 7)
-    middle = lax.reduce_precision(table - high, 8, 7)
-    low = table - high - middle
-    packed = jnp.concatenate([high, middle, low], axis=1).astype(jnp.bfloat16)
-    packed = jnp.pad(packed, ((0, 0), (0, LANES - 3 * experts)))
-    block = jnp.concatenate([head_out, packed], axis=1)
-    gain = norm_gain.astype(jnp.float32)
-    inverse = 1.0 / gain
-    scaled, mixture = layer(
-        n,
-        block,
-        residual.reshape(rows, n, cols).transpose(1, 0, 2),
-        gain.reshape(n, 1, cols),
-        inverse.reshape(n, 1, cols),
         out_weight,
         w_gate[0],
         w_up[0],
         w_down[0],
     )
-    hidden = scaled.transpose(1, 0, 2).reshape(rows, D).astype(jnp.float32) * inverse
-    return (hidden + mixture).astype(jnp.bfloat16)
 
 
 def solution(mesh):

time: 96.7 us -> 82.5 us (0.85)
  other arithmetic: 9.97 us -> 0 us
  matrix products: 6.26 us -> 0 us
  Pallas kernels: 75.1 us -> 76.7 us
    dot_general x3 -> x0, matrix products: 6.26 us -> none  [the longest x1 3.27 us: local_attention(): jnp.einsum('rhgt,thd->rhgd', weights, value_matrix, preferred_element_typ...]
    reduce_sum x4 -> x0, other arithmetic: 3.74 us -> none  [the longest x1 2.87 us: local_attention(): denominator = jnp.sum(raised, axis=-1) + own_raised]
    unnamed x18 -> x3, local copies, waits for them, and re-layouts: 1.03 us -> 4.27 us
    convert_element_type x3 -> x0, other arithmetic: 2.29 us -> none  [the longest x1 1.65 us: per_device(): return (hidden + mixture).astype(jnp.bfloat16)]
    reshape x5 -> x1, local copies, waits for them, and re-layouts: 3.04 us -> 1.31 us  [per_device(): norm_gain.reshape(1, -1)]
    pallas_call x1, Pallas kernels: 75.1 us -> 76.7 us  [layer(): pl.pallas_call(functools.partial(layer_kernel, n, chunks), out_shape=jax....]
where the time goes in v2:
time: 82.5 us; the launch traced here: 82.3 us
  Pallas kernels  76.7 us (93%)
  local copies, waits for them, and re-layouts  5.58 us (7%)
    pallas_call x1, Pallas kernels, layer(): pl.pallas_call(functools.partial(layer_kernel, n, chunks), out_shape=jax....  76.7 us
    unnamed x3, local copies, waits for them, and re-layouts  4.27 us

profile of v2, /device:TPU:0, one launch (start us, length us, event | category | flops | bytes accessed | tf_op | source)
XLA Modules:
  0.0 82.3 jit_solution(14237011345262149531)
XLA Ops:
  0.0 1.3 %copy.17.routes_ref = s32[16,2]{1,0:T(8,128)} copy(s32[16,2]{0,1:T(2,128)} %param.27) | data formatting | bytes 256 | tf_op args[11]
  1.3 1.3 %copy.18.route_weight_ref = f32[16,2]{1,0:T(8,128)} copy(f32[16,2]{0,1:T(2,128)} %param.28) | data formatting | bytes 256 | tf_op args[12]
  2.7 1.3 %reshape.7.gain_ref = bf16[1,4096]{1,0:T(2,128)(2,1)} reshape(bf16[4096]{0:T(1024)(128)(2,1)} %param.26) | data formatting | bytes 16384 | tf_op jit(solution)/shard_map/reshape | solution.py:631
  4.0 76.7 %shard_map.154 = bf16[16,4096]{1,0:T(8,128)(2,1)} custom-call(bf16[16,4096]{1,0:T(8,128)(2,1)} %query_ref.1, bf16[16,256]{1,0:T(8,128)(2,1)} %fresh_key_ref.1, bf16[16,256]{1,0:T(8,128)(2,1)} %fresh_value_ref.1, s32[1,16]{1,0:T(1,128)} %count_ref.1, s32[1,16]{1,0:T(1,128)} %bitcast.7, s32[1,32]{1,0:T(1,128)} %ranking_ref.1, bf16[16,4096]{1,0:T(8,128)(2,1)} %residual_ref.1, ...), custom_call_target="tpu_custom_call" | custom-call | flops 2952790016 | bytes 11534336 | tf_op jit(solution)/shard_map/pallas_call | solution.py:551
  80.7 1.6 %copy.20 = bf16[16,4096]{1,0:T(8,128)(2,1)} copy(bf16[16,4096]{1,0:T(8,128)(2,1)} %shard_map.154) | data formatting | bytes 262144

commit v3 on v2

--- a/solution.py
+++ b/solution.py
@@ -22,10 +22,14 @@
     lane = lax.broadcasted_iota(jnp.int32, (rows, LANES), 1)
     expert = lax.rem(lane, levels)
     table = jnp.zeros((rows, LANES), jnp.float32)
-    for t in range(routes_ref.shape[1]):
-        table += jnp.where(
-            routes_ref[:, t : t + 1] == expert, route_weight_ref[:, t : t + 1], 0.0
-        )
+    same = lax.broadcasted_iota(jnp.int32, (rows, rows), 0) == lax.broadcasted_iota(
+        jnp.int32, (rows, rows), 1
+    )
+    upright = lambda line: jnp.sum(jnp.where(same, line, 0.0), axis=1, keepdims=True)
+    for t in range(routes_ref.shape[0]):
+        route = upright(routes_ref[t : t + 1, :].astype(jnp.float32))
+        weight = upright(route_weight_ref[t : t + 1, :])
+        table += jnp.where(route == expert.astype(jnp.float32), weight, 0.0)
     high = table.astype(jnp.bfloat16).astype(jnp.float32)
     middle = (table - high).astype(jnp.bfloat16).astype(jnp.float32)
     low = table - high - middle
@@ -44,6 +48,7 @@
     values,
     by_head,
     out,
+    finished,
 ):
     f32 = jnp.float32
     rows = query_ref.shape[0]
@@ -103,6 +108,7 @@
         for h in range(heads):
             at = (g * heads + h) * HEAD_SIZE
             out[:, at : at + HEAD_SIZE] = mixed[h]
+        finished(g)
 
 
 def layer_kernel(
@@ -197,10 +203,127 @@
             barrier, inc=1, device_id={"expert": lax.rem(me + k, n)}, device_id_type=MESH
         )
 
+    def gather(buf, send, recv, slices, consume):
+        pieces = range(len(slices))
+
+        def copy(p, zz, yy, cc, way, target):
+            return pltpu.make_async_remote_copy(
+                src_ref=buf.at[(zz, yy, cc) + slices[p]],
+                dst_ref=buf.at[(zz, yy, cc) + slices[p]],
+                send_sem=send.at[p, way, zz, yy, cc],
+                recv_sem=recv.at[p, zz, yy, cc],
+                device_id={"expert": target},
+                device_id_type=MESH,
+            )
+
+        def up(p, zz):
+            return copy(p, zz, y, c, 0, device(jnp.minimum(z + 1, levels - 1), y, c))
+
+        def down(p, zz):
+            return copy(p, zz, y, c, 1, device(jnp.maximum(z - 1, 0), y, c))
+
+        def across(p, zz):
+            return copy(p, zz, y, c, 2, beside_y)
+
+        def beside(p, zz, yy):
+            return copy(p, zz, yy, c, 3, beside_core)
+
+        def landed(p, zz, yy, cc):
+            copy(p, zz, yy, cc, 3, beside_core).wait_recv()
+
+        def line(p, zz):
+            @pl.when((zz <= z) & (z < levels - 1))
+            def _():
+                up(p, zz).start()
+
+            @pl.when((zz >= z) & (z > 0))
+            def _():
+                down(p, zz).start()
+
+            across(p, zz).start()
+            beside(p, zz, y).start()
+
+        def along(p, zz):
+            landed(p, zz, y, c)
+            line(p, zz)
+
+        def crossed(p, zz):
+            landed(p, zz, 1 - y, c)
+            beside(p, zz, 1 - y).start()
+
+        def at_distance(distance, body):
+            @pl.loop(0, 2)
+            def _(sign):
+                zz = z - distance + 2 * distance * sign
+
+                @pl.when(
+                    (distance >= 0)
+                    & (zz >= 0)
+                    & (zz < levels)
+                    & ((distance > 0) | (sign == 0))
+                )
+                def _():
+                    body(zz)
+
+        def start(p):
+            line(p, z)
+
+        def relay():
+            if consume is not None:
+                consume(z, y, c)
+
+            @pl.loop(1, levels + 2)
+            def step(s):
+                for p in pieces:
+                    at_distance(s, functools.partial(along, p))
+                    at_distance(s - 1, functools.partial(crossed, p))
+                if consume is not None:
+                    at_distance(s, lambda zz: consume(zz, y, c))
+                    at_distance(s - 1, lambda zz: consume(zz, 1 - y, c))
+
+                def arrived(zz, yy):
+                    for p in pieces:
+                        landed(p, zz, yy, 1 - c)
+                    if consume is not None:
+                        consume(zz, yy, 1 - c)
+
+                at_distance(s - 1, lambda zz: arrived(zz, y))
+                at_distance(s - 2, lambda zz: arrived(zz, 1 - y))
+
+        def drain():
+            @pl.loop(0, levels)
+            def _(zz):
+                for p in pieces:
+
+                    @pl.when((zz <= z) & (z < levels - 1))
+                    def _():
+                        up(p, zz).wait_send()
+
+                    @pl.when((zz >= z) & (z > 0))
+                    def _():
+                        down(p, zz).wait_send()
+
+                    across(p, zz).wait_send()
+                    beside(p, zz, y).wait_send()
+                    beside(p, zz, 1 - y).wait_send()
+
+        return start, relay, drain
+
+    quarter = D // 4
+    columns = [(slice(None), pl.ds(p * quarter, quarter)) for p in range(3)]
+    columns.append((slice(None), pl.ds(3 * quarter, quarter + LANES)))
+    start1, relay1, drain1 = gather(g1, send1, recv1, columns, None)
+
+    def finished(g):
+        if g == 0:
+            pl.semaphore_wait(barrier, n - 1)
+        start1(2 * g)
+        start1(2 * g + 1)
+
     for d in range(n):
         at = slice(d * cols, (d + 1) * cols)
         residual_out[d] = residual_ref[:, at]
-        gains[d] = gain_ref[:, at].astype(jnp.float32)
+        gains[d] = gain_ref[at].astype(jnp.float32).reshape(1, cols)
         inverse[d] = 1.0 / gains[d]
     res[me] = residual_out[me]
     g1[z, y, c, :, D:] = packed_routes(levels, rows, routes_ref, route_weight_ref)
@@ -217,111 +340,8 @@
         values,
         by_head,
         g1.at[z, y, c],
+        finished,
     )
-    pl.semaphore_wait(barrier, n - 1)
-
-    def gather(buf, send, recv, consume, after_first):
-        def copy(zz, yy, cc, way, target):
-            return pltpu.make_async_remote_copy(
-                src_ref=buf.at[zz, yy, cc],
-                dst_ref=buf.at[zz, yy, cc],
-                send_sem=send.at[way, zz, yy, cc],
-                recv_sem=recv.at[zz, yy, cc],
-                device_id={"expert": target},
-                device_id_type=MESH,
-            )
-
-        def up(zz):
-            return copy(zz, y, c, 0, device(jnp.minimum(z + 1, levels - 1), y, c))
-
-        def down(zz):
-            return copy(zz, y, c, 1, device(jnp.maximum(z - 1, 0), y, c))
-
-        def across(zz):
-            return copy(zz, y, c, 2, beside_y)
-
-        def beside(zz, yy):
-            return copy(zz, yy, c, 3, beside_core)
-
-        def landed(zz, yy, cc):
-            copy(zz, yy, cc, 3, beside_core).wait_recv()
-
-        def line(zz):
-            @pl.when(zz != z)
-            def _():
-                landed(zz, y, c)
-
-            @pl.when((zz <= z) & (z < levels - 1))
-            def _():
-                up(zz).start()
-
-            @pl.when((zz >= z) & (z > 0))
-            def _():
-                down(zz).start()
-
-            across(zz).start()
-            beside(zz, y).start()
-
-        def at_distance(distance, body):
-            @pl.loop(0, 2)
-            def _(sign):
-                zz = z - distance + 2 * distance * sign
-
-                @pl.when(
-                    (distance >= 0)
-                    & (zz >= 0)
-                    & (zz < levels)
-                    & ((distance > 0) | (sign == 0))
-                )
-                def _():
-                    body(zz)
-
-        def crossed(zz):
-            landed(zz, 1 - y, c)
-            beside(zz, 1 - y).start()
-
-        @pl.loop(0, levels + 2)
-        def step(s):
-            at_distance(s, line)
-            at_distance(s - 1, crossed)
-
-            @pl.when(s == 0)
-            def _():
-                after_first()
-
-            if consume is not None:
-                at_distance(s, lambda zz: consume(zz, y, c))
-                at_distance(s - 1, lambda zz: consume(zz, 1 - y, c))
-
-            def near(zz):
-                landed(zz, y, 1 - c)
-                if consume is not None:
-                    consume(zz, y, 1 - c)
-
-            def far(zz):
-                landed(zz, 1 - y, 1 - c)
-                if consume is not None:
-                    consume(zz, 1 - y, 1 - c)
-
-            at_distance(s - 1, near)
-            at_distance(s - 2, far)
-
-        def drain():
-            @pl.loop(0, levels)
-            def _(zz):
-                @pl.when((zz <= z) & (z < levels - 1))
-                def _():
-                    up(zz).wait_send()
-
-                @pl.when((zz >= z) & (z > 0))
-                def _():
-                    down(zz).wait_send()
-
-                across(zz).wait_send()
-                beside(zz, y).wait_send()
-                beside(zz, 1 - y).wait_send()
-
-        return drain
 
     def residual_copy(k):
         return pltpu.make_async_remote_copy(
@@ -344,12 +364,11 @@
             device_id_type=MESH,
         ).wait_recv()
 
-    def send_residual():
-        @pl.loop(1, n)
-        def _(k):
-            residual_copy(k).start()
-
-    drain1 = gather(g1, send1, recv1, None, send_residual)
+    @pl.loop(1, n)
+    def _(k):
+        residual_copy(k).start()
+
+    relay1()
     weight_copies[0].wait()
 
     @pl.loop(1, n)
@@ -380,11 +399,14 @@
         plain = block.astype(jnp.float32) * inverse[d]
         squares[...] += jnp.sum(plain * plain, axis=1, keepdims=True)
 
-    def wait_weights():
-        weight_copies[1].wait()
-        weight_copies[2].wait()
-
-    drain2 = gather(g2, send2, recv2, consume, wait_weights)
+    share = total // 4
+    strips = [(pl.ds(p * share, share), slice(None)) for p in range(4)]
+    start2, relay2, drain2 = gather(g2, send2, recv2, strips, consume)
+    for p in range(4):
+        start2(p)
+    weight_copies[1].wait()
+    weight_copies[2].wait()
+    relay2()
     scale = lax.rsqrt(squares[...] * (1.0 / D) + 1e-06)
     gated = gate[...] * scale
     act[...] = (gated / (1.0 + jnp.exp(-gated)) * (upward[...] * scale)).astype(jnp.bfloat16)
@@ -414,18 +436,25 @@
             device_id_type=MESH,
         )
 
-    def z_copy(j, goal, slot, target):
+    def z_copy(j, goal):
         return pltpu.make_async_remote_copy(
             src_ref=part.at[j, c, y, goal],
-            dst_ref=from_z.at[j, slot],
+            dst_ref=from_z.at[j, z],
             send_sem=z_send.at[j, goal],
-            recv_sem=z_recv.at[j, slot],
-            device_id={"expert": target},
+            recv_sem=z_recv.at[j, z],
+            device_id={"expert": device(goal, y, c)},
             device_id_type=MESH,
         )
 
-    def z_landed(j, slot):
-        z_copy(j, 0, slot, beside_y).wait_recv()
+    def z_landed(j, source):
+        pltpu.make_async_remote_copy(
+            src_ref=part.at[j, c, y, source],
+            dst_ref=from_z.at[j, source],
+            send_sem=z_send.at[j, source],
+            recv_sem=z_recv.at[j, source],
+            device_id={"expert": device(source, y, c)},
+            device_id_type=MESH,
+        ).wait_recv()
 
     def multiply(j):
         value = jnp.dot(
@@ -453,44 +482,20 @@
             part[j, c, y].astype(jnp.float32) + from_y[j].astype(jnp.float32)
         ).astype(jnp.bfloat16)
 
-    def chain(j, rising):
-        count = jnp.where(rising, levels - 1 - z, z)
-        first = jnp.where(rising, z == 0, z == levels - 1)
-        target = device(jnp.where(rising, z + 1, z - 1), y, c)
-
-        @pl.loop(0, count)
+    def scatter(j):
+        @pl.loop(1, levels)
         def _(k):
-            goal = jnp.where(rising, levels - 1 - k, k)
-
-            @pl.when(jnp.logical_not(first))
-            def _():
-                z_landed(j, goal)
-                part[j, c, y, goal] = (
-                    part[j, c, y, goal].astype(jnp.float32)
-                    + from_z[j, goal].astype(jnp.float32)
-                ).astype(jnp.bfloat16)
-
-            last_down = jnp.logical_not(rising) & (goal == z - 1)
-            z_copy(j, goal, jnp.where(last_down, levels, goal), target).start()
-
-    def chains(j):
-        rising = z < levels // 2
-        chain(j, rising)
-        chain(j, jnp.logical_not(rising))
+            z_copy(j, lax.rem(z + k, levels)).start()
 
     def finish(j):
         at = pl.ds(pl.multiple_of(j * width, width), width)
         hidden_own[:, at] += part[j, c, y, z].astype(jnp.float32)
 
-        @pl.when(z > 0)
-        def _():
-            z_landed(j, z)
-            hidden_own[:, at] += from_z[j, z].astype(jnp.float32)
-
-        @pl.when(z < levels - 1)
-        def _():
-            z_landed(j, levels)
-            hidden_own[:, at] += from_z[j, levels].astype(jnp.float32)
+        @pl.loop(1, levels)
+        def _(k):
+            source = lax.rem(z + k, levels)
+            z_landed(j, source)
+            hidden_own[:, at] += from_z[j, source].astype(jnp.float32)
 
         out_ref[:, at] = hidden_own[:, at].astype(jnp.bfloat16)
 
@@ -511,7 +516,7 @@
     @pl.loop(0, chunks)
     def _(j):
         add_y(j)
-        chains(j)
+        scatter(j)
 
     @pl.loop(0, chunks)
     def _(j):
@@ -533,7 +538,7 @@
         def _(goal):
             @pl.when(goal != z)
             def _():
-                z_copy(j, goal, goal, beside_y).wait_send()
+                z_copy(j, goal).wait_send()
 
 
 def layer(n, *operands):
@@ -575,12 +580,12 @@
             pltpu.VMEM((chunks, 2, 2, levels, rows, width), bf16),
             pltpu.VMEM((chunks, 2, levels, rows, width), bf16),
             pltpu.VMEM((chunks, levels, rows, width), bf16),
-            pltpu.VMEM((chunks, levels + 1, rows, width), bf16),
+            pltpu.VMEM((chunks, levels, rows, width), bf16),
             dma((6,)),
+            dma((4, 4, levels, 2, 2)),
             dma((4, levels, 2, 2)),
-            dma((levels, 2, 2)),
+            dma((4, 4, levels, 2, 2)),
             dma((4, levels, 2, 2)),
-            dma((levels, 2, 2)),
             dma((n,)),
             dma((n,)),
             dma((chunks,)),
@@ -588,7 +593,7 @@
             dma((chunks,)),
             dma((chunks,)),
             dma((chunks, levels)),
-            dma((chunks, levels + 1)),
+            dma((chunks, levels)),
         ],
         compiler_params=pltpu.CompilerParams(
             collective_id=0, has_side_effects=True, vmem_limit_bytes=62 * 1024 * 1024
@@ -628,9 +633,9 @@
         last_page_fill.reshape(1, -1),
         local_page_ranking,
         residual,
-        norm_gain.reshape(1, -1),
-        routes,
-        route_weight,
+        norm_gain,
+        routes.T,
+        route_weight.T,
         key_cache_pages,
         value_cache_pages,
         out_weight,

time: 82.5 us -> 70.6 us (0.86)
  Pallas kernels: 76.7 us -> 68.8 us
  local copies, waits for them, and re-layouts: 5.58 us -> 1.57 us
    pallas_call x1, Pallas kernels: 76.7 us -> 68.8 us  [layer(): pl.pallas_call(functools.partial(layer_kernel, n, chunks), out_shape=jax....]
    unnamed x3 -> x1, local copies, waits for them, and re-layouts: 4.27 us -> 1.57 us
    reshape x1 -> x0, local copies, waits for them, and re-layouts: 1.31 us -> none  [per_device(): norm_gain.reshape(1, -1)]
where the time goes in v3:
time: 70.6 us; the launch traced here: 70.4 us
  Pallas kernels  68.8 us (97%)
  local copies, waits for them, and re-layouts  1.57 us (2%)
    pallas_call x1, Pallas kernels, layer(): pl.pallas_call(functools.partial(layer_kernel, n, chunks), out_shape=jax....  68.8 us
    unnamed x1, local copies, waits for them, and re-layouts  1.57 us

profile of v3, /device:TPU:0, one launch (start us, length us, event | category | flops | bytes accessed | tf_op | source)
XLA Modules:
  0.0 70.4 jit_solution(15338279909784333643)
XLA Ops:
  0.0 68.8 %shard_map.154 = bf16[16,4096]{1,0:T(8,128)(2,1)} custom-call(bf16[16,4096]{1,0:T(8,128)(2,1)} %query_ref.1, bf16[16,256]{1,0:T(8,128)(2,1)} %fresh_key_ref.1, bf16[16,256]{1,0:T(8,128)(2,1)} %fresh_value_ref.1, s32[1,16]{1,0:T(1,128)} %count_ref.1, s32[1,16]{1,0:T(1,128)} %bitcast.11, s32[1,32]{1,0:T(1,128)} %ranking_ref.1, bf16[16,4096]{1,0:T(8,128)(2,1)} %residual_ref.1, ...), custom_call_target="tpu_custom_call" | custom-call | flops 2952790016 | bytes 11534336 | tf_op jit(solution)/shard_map/pallas_call | solution.py:556
  68.9 1.6 %copy.18 = bf16[16,4096]{1,0:T(8,128)(2,1)} copy(bf16[16,4096]{1,0:T(8,128)(2,1)} %shard_map.154) | data formatting | bytes 262144

commit v4 on v3

--- a/solution.py
+++ b/solution.py
@@ -309,16 +309,14 @@
 
         return start, relay, drain
 
-    quarter = D // 4
-    columns = [(slice(None), pl.ds(p * quarter, quarter)) for p in range(3)]
-    columns.append((slice(None), pl.ds(3 * quarter, quarter + LANES)))
+    half = D // 2
+    columns = [(slice(None), pl.ds(0, half)), (slice(None), pl.ds(half, half + LANES))]
     start1, relay1, drain1 = gather(g1, send1, recv1, columns, None)
 
     def finished(g):
         if g == 0:
             pl.semaphore_wait(barrier, n - 1)
-        start1(2 * g)
-        start1(2 * g + 1)
+        start1(g)
 
     for d in range(n):
         at = slice(d * cols, (d + 1) * cols)
@@ -399,10 +397,10 @@
         plain = block.astype(jnp.float32) * inverse[d]
         squares[...] += jnp.sum(plain * plain, axis=1, keepdims=True)
 
-    share = total // 4
-    strips = [(pl.ds(p * share, share), slice(None)) for p in range(4)]
+    share = total // 2
+    strips = [(pl.ds(p * share, share), slice(None)) for p in range(2)]
     start2, relay2, drain2 = gather(g2, send2, recv2, strips, consume)
-    for p in range(4):
+    for p in range(2):
         start2(p)
     weight_copies[1].wait()
     weight_copies[2].wait()
@@ -582,10 +580,10 @@
             pltpu.VMEM((chunks, levels, rows, width), bf16),
             pltpu.VMEM((chunks, levels, rows, width), bf16),
             dma((6,)),
-            dma((4, 4, levels, 2, 2)),
-            dma((4, levels, 2, 2)),
-            dma((4, 4, levels, 2, 2)),
-            dma((4, levels, 2, 2)),
+            dma((2, 4, levels, 2, 2)),
+            dma((2, levels, 2, 2)),
+            dma((2, 4, levels, 2, 2)),
+            dma((2, levels, 2, 2)),
             dma((n,)),
             dma((n,)),
             dma((chunks,)),

time: 70.6 us -> 69.3 us (0.982)
  Pallas kernels: 68.8 us -> 67.6 us
    pallas_call x1, Pallas kernels: 68.8 us -> 67.6 us  [layer(): pl.pallas_call(functools.partial(layer_kernel, n, chunks), out_shape=jax....]
where the time goes in v4:
time: 69.3 us; the launch traced here: 69.2 us
  Pallas kernels  67.6 us (98%)
  local copies, waits for them, and re-layouts  1.57 us (2%)
    pallas_call x1, Pallas kernels, layer(): pl.pallas_call(functools.partial(layer_kernel, n, chunks), out_shape=jax....  67.6 us
    unnamed x1, local copies, waits for them, and re-layouts  1.57 us

profile of v4, /device:TPU:0, one launch (start us, length us, event | category | flops | bytes accessed | tf_op | source)
XLA Modules:
  0.0 69.2 jit_solution(17248016088856562325)
XLA Ops:
  0.0 67.6 %shard_map.154 = bf16[16,4096]{1,0:T(8,128)(2,1)} custom-call(bf16[16,4096]{1,0:T(8,128)(2,1)} %query_ref.1, bf16[16,256]{1,0:T(8,128)(2,1)} %fresh_key_ref.1, bf16[16,256]{1,0:T(8,128)(2,1)} %fresh_value_ref.1, s32[1,16]{1,0:T(1,128)} %count_ref.1, s32[1,16]{1,0:T(1,128)} %bitcast.11, s32[1,32]{1,0:T(1,128)} %ranking_ref.1, bf16[16,4096]{1,0:T(8,128)(2,1)} %residual_ref.1, ...), custom_call_target="tpu_custom_call" | custom-call | flops 2952790016 | bytes 11534336 | tf_op jit(solution)/shard_map/pallas_call | solution.py:554
  67.6 1.6 %copy.18 = bf16[16,4096]{1,0:T(8,128)(2,1)} copy(bf16[16,4096]{1,0:T(8,128)(2,1)} %shard_map.154) | data formatting | bytes 262144
